TPU v7x, 32 devices: a whole 2x2x4 slice. The times are simulated.
32 devices in a mesh: space: 4 (over y, x), tm: 8 (over z, core).
Axes of the slice: x: 2, y: 2, z: 4, core: 2. Of those that a mesh axis runs over, the one named last changes fastest.
Arguments:
- lattice_field: float32 [32, 16, 2048], P('tm', 'space'), may hold values from -6 to 6
- parity: int32 [8, 4, 128], P('tm', 'space'), may hold values from 0 to 1
- block_list: int32 [8, 8], replicated, may hold values from 0 to 7, as said below
- w_embed: bfloat16 [256, 768], replicated, may hold values from -0.5 to 0.5
- b_embed: float32 [768], replicated, may hold values from -3 to 3
- gain_in: float32 [768], replicated, may hold values from 0.5 to 1.5
- w_qkv: bfloat16 [768, 2304], replicated, may hold values from -4 to 4
- gain_out: float32 [768], replicated, may hold values from 0.5 to 1.5
- w_head: bfloat16 [768, 512], replicated, may hold values from -0.21875 to 0.21875
- b_head: float32 [512], replicated, may hold values from -3 to 3
Outputs:
- new_field: float32 [32, 16, 2048], P('tm', 'space')
- action_density: float32 [32, 16, 2048], P('tm', 'space')
- time_link: float32 [32, 16, 2048], P('tm', 'space')
- slab_link: float32 [32, 16, 2048], P('tm', 'space')
- totals: float32 [2], replicated
Inputs may be any that keep to these rules, and one draw needn't show every extreme that they name: `block_list`: row b lists 8 different block numbers, b among them.
All inputs are finite; a program needn't handle non-finite values.
Results may differ from a plain program's by a relative error of at most 0.006.
Values may be sent and summed in bfloat16 or wider, within the bound.
A program may use at most 64 MiB of HBM per device.

v0:
```python
import math

import jax
import jax.numpy as jnp
from jax import lax
from jax.sharding import PartitionSpec as P

P_SIZE = 4
D = 768
HEADS = 12
HS = 64
LY = 32
LZ = 64
BLK = 128


hopping = 0.2
quartic = 0.5
epsilon = 1e-05
log_two_pi = math.log(2.0 * math.pi)
floor_score = -1e30


def shifted(x, axis, by):
    length = lax.axis_size(axis)
    return lax.ppermute(x, axis, [(i, (i + by) % length) for i in range(length)])


def layer_norm(values, gain_vec):
    centre = values - jnp.mean(values, axis=-1, keepdims=True)
    spread = jnp.mean(centre * centre, axis=-1, keepdims=True)
    return centre * lax.rsqrt(spread + epsilon) * gain_vec


def site_parity(patch_side):
    positions = jnp.arange(patch_side**4, dtype=jnp.int32)
    return (
        positions // patch_side**3
        + positions // patch_side**2 % patch_side
        + positions // patch_side % patch_side
        + positions % patch_side
    ) % 2


def embed_rows(frozen_in, w_embed, b_embed, gain_in):
    embedded = jnp.dot(frozen_in, w_embed, preferred_element_type=jnp.float32) + b_embed
    return (embedded, layer_norm(embedded, gain_in).astype(jnp.bfloat16))


def attend(carry_in, queries, key_part, value_part, first_key, block_rows):
    running_max, running_sum, running_out = carry_in
    key_rows = key_part.shape[0]
    key_block = (first_key + jnp.arange(key_rows, dtype=jnp.int32)) // BLK
    listed = jnp.any(block_rows[:, :, None] == key_block[None, None, :], axis=1)
    allowed = jnp.repeat(listed, BLK, axis=0)[None]
    query_heads = queries.reshape(queries.shape[0], HEADS, HS)
    scores = jnp.einsum(
        "qhd,khd->hqk",
        query_heads,
        key_part.reshape(key_rows, HEADS, HS),
        preferred_element_type=jnp.float32,
    ) * HS ** (-0.5)
    masked = jnp.where(allowed, scores, floor_score)
    new_max = jnp.maximum(running_max, jnp.max(masked, axis=2))
    exp_scores = jnp.where(allowed, jnp.exp(scores - new_max[:, :, None]), 0.0)
    factor = jnp.exp(running_max - new_max)
    running_sum = running_sum * factor + jnp.sum(exp_scores, axis=2)
    product = jnp.einsum(
        "hqk,khd->hqd",
        exp_scores.astype(jnp.bfloat16),
        value_part.reshape(key_rows, HEADS, HS),
        preferred_element_type=jnp.float32,
    )
    running_out = running_out * factor[:, :, None] + product
    return (new_max, running_sum, running_out)


def fold_rows(carry_in, pieces_in, make_pair, queries, block_rows):
    row_total = pieces_in[0].shape[0]
    pieces_split = tuple(
        (
            piece_arr.reshape((row_total // BLK, BLK) + piece_arr.shape[1:])
            for piece_arr in pieces_in
        )
    )

    def visit_block(carry_now, item_pair):
        position, block_parts = item_pair
        first_key = position * BLK
        block_id = first_key // BLK
        needed = jnp.any(block_rows == block_id)

        def compute_block(carry_here):
            key_part, value_part = make_pair(block_parts)
            return attend(carry_here, queries, key_part, value_part, first_key, block_rows)

        def skip_block(carry_here):
            return carry_here

        return (lax.cond(needed, compute_block, skip_block, carry_now), None)

    carry_out, _ = lax.scan(
        visit_block, carry_in, (jnp.arange(row_total // BLK, dtype=jnp.int32), pieces_split)
    )
    return carry_out


def shards(
    lattice_field, parity, block_list, w_embed, b_embed, gain_in, w_qkv, gain_out, w_head, b_head
):
    tokens_dev = LY // P_SIZE * (LZ // P_SIZE)
    patch_len = P_SIZE**4
    lattice_grid = lattice_field.reshape(
        P_SIZE, P_SIZE, LY // P_SIZE, P_SIZE, LZ // P_SIZE, P_SIZE
    ).transpose(2, 4, 0, 1, 3, 5)
    site_rows = lattice_grid.reshape(tokens_dev, patch_len)
    frozen = site_parity(P_SIZE)[None, :] == parity.reshape(tokens_dev)[:, None]
    frozen_in = jnp.where(frozen, site_rows, 0.0).astype(jnp.bfloat16)
    embedded, normed = embed_rows(frozen_in, w_embed, b_embed, gain_in)
    blocks_dev = tokens_dev // BLK
    block_rows = lax.dynamic_slice_in_dim(
        block_list, lax.axis_index("tm") * blocks_dev, blocks_dev, 0
    )
    start_state = (
        jnp.full((HEADS, tokens_dev), floor_score, jnp.float32),
        jnp.zeros((HEADS, tokens_dev), jnp.float32),
        jnp.zeros((HEADS, tokens_dev, HS), jnp.float32),
    )
    qkv_rows = jnp.dot(normed, w_qkv, preferred_element_type=jnp.float32).astype(jnp.bfloat16)
    queries = qkv_rows[:, :D]

    def from_pair(block_parts):
        return (block_parts[0], block_parts[1])

    result = fold_rows(
        start_state,
        (
            lax.all_gather(qkv_rows[:, D : 2 * D], "tm", axis=0, tiled=True),
            lax.all_gather(qkv_rows[:, 2 * D :], "tm", axis=0, tiled=True),
        ),
        from_pair,
        queries,
        block_rows,
    )
    _, running_sum, running_out = result
    mixed = (running_out / running_sum[:, :, None]).transpose(1, 0, 2).reshape(tokens_dev, D)
    hidden = embedded + mixed
    normed_out = layer_norm(hidden, gain_out).astype(jnp.bfloat16)
    affine = jnp.dot(normed_out, w_head, preferred_element_type=jnp.float32) + b_head
    scale_log = jnp.tanh(affine[:, :patch_len])
    shift_val = affine[:, patch_len:]
    moved = jnp.where(frozen, site_rows, site_rows * jnp.exp(scale_log) + shift_val)
    log_det = jnp.sum(jnp.where(frozen, 0.0, scale_log))
    new_field = (
        moved.reshape(LY // P_SIZE, LZ // P_SIZE, P_SIZE, P_SIZE, P_SIZE, P_SIZE)
        .transpose(2, 3, 0, 4, 1, 5)
        .reshape(P_SIZE, P_SIZE, LY * LZ)
    )
    ahead_time = shifted(new_field[0:1].astype(jnp.bfloat16), "tm", -1).astype(jnp.float32)
    ahead_slab = shifted(new_field[:, 0:1].astype(jnp.bfloat16), "space", -1).astype(jnp.float32)
    next_time_field = jnp.concatenate([new_field[1:], ahead_time], axis=0)
    next_slab_field = jnp.concatenate([new_field[:, 1:], ahead_slab], axis=1)
    cube = new_field.reshape(P_SIZE, P_SIZE, LY, LZ)
    next_y_field = jnp.roll(cube, -1, 2).reshape(P_SIZE, P_SIZE, LY * LZ)
    next_z_field = jnp.roll(cube, -1, 3).reshape(P_SIZE, P_SIZE, LY * LZ)
    neighbours = next_time_field + next_slab_field
    neighbours = neighbours + next_y_field
    neighbours = neighbours + next_z_field
    squared = new_field * new_field
    density = (
        -2.0 * hopping * new_field * neighbours
        + squared
        + quartic * (squared - 1.0) * (squared - 1.0)
    )
    time_link = new_field * next_time_field
    slab_link = new_field * next_slab_field
    local_log = -0.5 * jnp.sum(lattice_field * lattice_field) - log_det
    local_act = jnp.sum(density)
    sum_log, sum_act = lax.psum((local_log, local_act), ("space", "tm"))
    site_count = lattice_field.size * lax.axis_size("space") * lax.axis_size("tm")
    totals = jnp.stack([sum_log / site_count - 0.5 * log_two_pi, sum_act / site_count]).astype(
        jnp.float32
    )
    return (new_field, density, time_link, slab_link, totals)


def solution(mesh):
    in_specs = (
        P("tm", "space", None),
        P("tm", "space", None),
        P(),
        P(),
        P(),
        P(),
        P(),
        P(),
        P(),
        P(),
    )
    out_specs = (
        P("tm", "space", None),
        P("tm", "space", None),
        P("tm", "space", None),
        P("tm", "space", None),
        P(),
    )
    return jax.shard_map(shards, mesh=mesh, in_specs=in_specs, out_specs=out_specs, check_vma=False)
```

profile of v0, /device:TPU:0, one launch (start us, length us, event | category | flops | bytes accessed | tf_op | source)
XLA Modules:
  0.0 311.5 jit_solution(11542457833670575003)
XLA Ops:
  7.3 6.7 %reshape.277 = f32[4,4,8,4,16,4]{5,4,3,2,1,0:T(8,128)} reshape(f32[4,4,2048]{2,1,0:T(4,128)} %param.14) | data formatting | bytes 262144 | tf_op jit(solution)/shard_map/reshape | solution.py:113
  14.0 5.7 %copy.48 = f32[8,16,4,4,4,4]{1,0,5,4,3,2:T(8,128)} copy(f32[8,16,4,4,4,4]{5,1,4,0,3,2:T(8,128)} %bitcast.53) | data formatting | bytes 262144 | tf_op jit(solution)/shard_map/transpose | solution.py:115
  33.2 22.0 %all-gather.3.cloned.1.call-done = bf16[1024,768]{1,0:T(8,128)(2,1)} async-done(((bf16[128,768]{1,0:T(8,128)(2,1)}), bf16[1024,768]{1,0:T(8,128)(2,1)}) %all-gather.3.cloned.1.call-update) | async-done | bytes 1572880 | tf_op jit(solution)/shard_map/all_gather | solution.py:138
  55.1 2.6 copy.50
  57.7 23.7 %all-gather.5.cloned.1.call-done = bf16[1024,768]{1,0:T(8,128)(2,1)} async-done(((bf16[128,768]{1,0:T(8,128)(2,1)}), bf16[1024,768]{1,0:T(8,128)(2,1)}) %all-gather.5.cloned.1.call-update) | async-done | bytes 1572880 | tf_op jit(solution)/shard_map/all_gather | solution.py:139
  81.4 2.6 copy.52
  85.3 65.4 %while.16 = (s32[]{:T(128)}, f32[12,128]{1,0:T(8,128)S(1)}, f32[12,128]{1,0:T(8,128)S(1)}, f32[12,128,64]{1,2,0:T(8,128)}, s32[8]{0:T(128)}, /*index=5*/s32[1,8]...) while((s32[]{:T(128)}, f32[12,128]{1,0:T(8,128)S(1)}, ...), condition=%wide.region_9.10_spmd, body=%wide.region_2.9_spmd.sunk | while | flops 52304800 | bytes 7768141 | solution.py:102
  89.0 4.5 %conditional.2 = ((f32[12,128]{1,0:T(8,128)S(1)}, f32[12,128]{1,0:T(8,128)S(1)}, f32[12,128,64]{1,2,0:T(8,128)})) conditional(s32[]{:T(128)} %convert_element_type.60, (f32[12,128]{1,0:T(8,128)S(1)}, f32[12,128]{1,0:T(8,128)S(1)}, f32[12,128,64]{1,2,0:T(8,128)}) %tuple.58, (s32[1,8]{1,0:T(1,128)}, s32[]{:T(128)}, bf16[8,128,768]{1,2,0:T(8,128)(2,1)}, ...), branch_computations={%region_4.4_spmd, %region_5.8_spmd} | conditional | flops 52304768 | bytes 7767680 | solution.py:100
  97.2 4.5 %conditional.2 = ((f32[12,128]{1,0:T(8,128)S(1)}, f32[12,128]{1,0:T(8,128)S(1)}, f32[12,128,64]{1,2,0:T(8,128)})) conditional(s32[]{:T(128)} %convert_element_type.60, (f32[12,128]{1,0:T(8,128)S(1)}, f32[12,128]{1,0:T(8,128)S(1)}, f32[12,128,64]{1,2,0:T(8,128)}) %tuple.58, (s32[1,8]{1,0:T(1,128)}, s32[]{:T(128)}, bf16[8,128,768]{1,2,0:T(8,128)(2,1)}, ...), branch_computations={%region_4.4_spmd, %region_5.8_spmd} | conditional | flops 52304768 | bytes 7767680 | solution.py:100
  105.3 4.5 %conditional.2 = ((f32[12,128]{1,0:T(8,128)S(1)}, f32[12,128]{1,0:T(8,128)S(1)}, f32[12,128,64]{1,2,0:T(8,128)})) conditional(s32[]{:T(128)} %convert_element_type.60, (f32[12,128]{1,0:T(8,128)S(1)}, f32[12,128]{1,0:T(8,128)S(1)}, f32[12,128,64]{1,2,0:T(8,128)}) %tuple.58, (s32[1,8]{1,0:T(1,128)}, s32[]{:T(128)}, bf16[8,128,768]{1,2,0:T(8,128)(2,1)}, ...), branch_computations={%region_4.4_spmd, %region_5.8_spmd} | conditional | flops 52304768 | bytes 7767680 | solution.py:100
  113.5 4.5 %conditional.2 = ((f32[12,128]{1,0:T(8,128)S(1)}, f32[12,128]{1,0:T(8,128)S(1)}, f32[12,128,64]{1,2,0:T(8,128)})) conditional(s32[]{:T(128)} %convert_element_type.60, (f32[12,128]{1,0:T(8,128)S(1)}, f32[12,128]{1,0:T(8,128)S(1)}, f32[12,128,64]{1,2,0:T(8,128)}) %tuple.58, (s32[1,8]{1,0:T(1,128)}, s32[]{:T(128)}, bf16[8,128,768]{1,2,0:T(8,128)(2,1)}, ...), branch_computations={%region_4.4_spmd, %region_5.8_spmd} | conditional | flops 52304768 | bytes 7767680 | solution.py:100
  121.7 4.5 %conditional.2 = ((f32[12,128]{1,0:T(8,128)S(1)}, f32[12,128]{1,0:T(8,128)S(1)}, f32[12,128,64]{1,2,0:T(8,128)})) conditional(s32[]{:T(128)} %convert_element_type.60, (f32[12,128]{1,0:T(8,128)S(1)}, f32[12,128]{1,0:T(8,128)S(1)}, f32[12,128,64]{1,2,0:T(8,128)}) %tuple.58, (s32[1,8]{1,0:T(1,128)}, s32[]{:T(128)}, bf16[8,128,768]{1,2,0:T(8,128)(2,1)}, ...), branch_computations={%region_4.4_spmd, %region_5.8_spmd} | conditional | flops 52304768 | bytes 7767680 | solution.py:100
  129.9 4.5 %conditional.2 = ((f32[12,128]{1,0:T(8,128)S(1)}, f32[12,128]{1,0:T(8,128)S(1)}, f32[12,128,64]{1,2,0:T(8,128)})) conditional(s32[]{:T(128)} %convert_element_type.60, (f32[12,128]{1,0:T(8,128)S(1)}, f32[12,128]{1,0:T(8,128)S(1)}, f32[12,128,64]{1,2,0:T(8,128)}) %tuple.58, (s32[1,8]{1,0:T(1,128)}, s32[]{:T(128)}, bf16[8,128,768]{1,2,0:T(8,128)(2,1)}, ...), branch_computations={%region_4.4_spmd, %region_5.8_spmd} | conditional | flops 52304768 | bytes 7767680 | solution.py:100
  138.0 4.5 %conditional.2 = ((f32[12,128]{1,0:T(8,128)S(1)}, f32[12,128]{1,0:T(8,128)S(1)}, f32[12,128,64]{1,2,0:T(8,128)})) conditional(s32[]{:T(128)} %convert_element_type.60, (f32[12,128]{1,0:T(8,128)S(1)}, f32[12,128]{1,0:T(8,128)S(1)}, f32[12,128,64]{1,2,0:T(8,128)}) %tuple.58, (s32[1,8]{1,0:T(1,128)}, s32[]{:T(128)}, bf16[8,128,768]{1,2,0:T(8,128)(2,1)}, ...), branch_computations={%region_4.4_spmd, %region_5.8_spmd} | conditional | flops 52304768 | bytes 7767680 | solution.py:100
  146.2 4.5 %conditional.2 = ((f32[12,128]{1,0:T(8,128)S(1)}, f32[12,128]{1,0:T(8,128)S(1)}, f32[12,128,64]{1,2,0:T(8,128)})) conditional(s32[]{:T(128)} %convert_element_type.60, (f32[12,128]{1,0:T(8,128)S(1)}, f32[12,128]{1,0:T(8,128)S(1)}, f32[12,128,64]{1,2,0:T(8,128)}) %tuple.58, (s32[1,8]{1,0:T(1,128)}, s32[]{:T(128)}, bf16[8,128,768]{1,2,0:T(8,128)(2,1)}, ...), branch_computations={%region_4.4_spmd, %region_5.8_spmd} | conditional | flops 52304768 | bytes 7767680 | solution.py:100
  163.4 5.4 %copy.57 = f32[4,4,8,4,16,4]{5,4,3,2,1,0:T(8,128)} copy(f32[4,4,8,4,16,4]{4,2,5,3,1,0:T(8,128)} %bitcast.54) | data formatting | bytes 262144 | tf_op jit(solution)/shard_map/transpose | solution.py:156
  168.9 5.6 %reshape.283 = f32[4,4,2048]{2,1,0:T(4,128)} reshape(f32[4,4,8,4,16,4]{5,4,3,2,1,0:T(8,128)} %copy.57) | data formatting | bytes 262144 | tf_op jit(solution)/shard_map/reshape | solution.py:157
  174.4 4.3 %reshape_reshape.3 = f32[4,4,32,64]{3,2,1,0:T(8,128)} reshape(f32[4,4,8,4,16,4]{5,4,3,2,1,0:T(8,128)} %copy.57) | data formatting | bytes 262144 | tf_op jit(solution)/shard_map/reshape;reshape | solution.py:163
  189.2 2.5 copy.59
  204.6 4.4 %reshape.287 = f32[4,4,8,4,16,4]{5,4,3,2,1,0:T(8,128)} reshape(f32[4,4,32,64]{3,2,1,0:T(8,128)} %pad_maximum_fusion.1) | data formatting | bytes 262144 | tf_op jit(solution)/shard_map/reshape | solution.py:165
  210.8 4.5 %reshape.286 = f32[4,4,8,4,16,4]{5,4,3,2,1,0:T(8,128)} reshape(f32[4,4,32,64]{3,2,1,0:T(8,128)} %pad_maximum_fusion) | data formatting | bytes 262144 | tf_op jit(solution)/shard_map/reshape | solution.py:164
  215.3 4.6 %copy.58 = f32[3,4,8,4,16,4]{5,4,3,2,1,0:T(8,128)} copy(f32[3,4,8,4,16,4]{4,2,5,3,1,0:T(8,128)} %slice.68) | data formatting | bytes 196608 | tf_op jit(solution)/shard_map/slice | solution.py:161
  219.8 5.7 %copy.66 = f32[4,4,8,4,16,4]{4,2,5,3,1,0:T(8,128)} copy(f32[4,4,8,4,16,4]{5,4,3,2,1,0:T(8,128)} %reshape.287) | data formatting | bytes 262144 | tf_op jit(solution)/shard_map/reshape | solution.py:165
  225.5 5.6 %copy.65 = f32[4,4,8,4,16,4]{4,2,5,3,1,0:T(8,128)} copy(f32[4,4,8,4,16,4]{5,4,3,2,1,0:T(8,128)} %reshape.286) | data formatting | bytes 262144 | tf_op jit(solution)/shard_map/reshape | solution.py:164
  231.2 5.1 %reshape.288 = f32[4,3,8,4,16,4]{5,4,3,2,1,0:T(8,128)} reshape(f32[4,3,2048]{2,1,0:T(4,128)} %slice.70) | data formatting | bytes 196608 | tf_op jit(solution)/shard_map/concatenate | solution.py:162
  236.3 4.6 %copy.63 = f32[4,3,8,4,16,4]{4,2,5,3,1,0:T(8,128)} copy(f32[4,3,8,4,16,4]{5,4,3,2,1,0:T(8,128)} %reshape.288) | data formatting | bytes 196608 | tf_op jit(solution)/shard_map/concatenate | solution.py:162
  243.6 2.8 copy.61
  247.8 2.8 concatenate.33
  250.7 2.8 copy.64
  253.5 3.7 %fusion.5 = f32[]{:T(128)} fusion(f32[4,4,8,4,16,4]{4,2,5,3,1,0:T(8,128)} %copy.66, f32[4,4,8,4,16,4]{4,2,5,3,1,0:T(8,128)} %copy.65, f32[1,4,8,4,16,4]{4,2,5,3,1,0:T(8,128)} %copy.61, f32[3,4,8,4,16,4]{4,2,5,3,1,0:T(8,128)} %slice.68, f32[4,1,8,4,16,4]{4,2,5,3,1,0:T(8,128)} %copy.64, f32[4,3,8,4,16,4]{4,2,5,3,1,0:T(8,128)} %copy.63, ...), kind=kLoop, calls=%fused_computation.25 | loop fusion | flops 458751 | bytes 655364 | tf_op jit(solution)/shard_map/reduce_sum | solution.py:178
  257.2 4.6 %slice.55 = f32[3,4,2048]{2,1,0:T(4,128)} reshape(f32[3,4,8,4,16,4]{5,4,3,2,1,0:T(8,128)} %copy.58) | data formatting | bytes 196608 | tf_op jit(solution)/shard_map/slice | solution.py:161
  261.8 38.1 %all-reduce = (f32[]{:T(128)}, f32[]{:T(128)}) all-reduce(f32[]{:T(128)} %fusion.5, f32[]{:T(128)S(6)} %sub.78), channel_id=1, replica_groups=mesh['space'=4,'tm'=8] {'space','tm'}, use_global_device_ids=true, to_apply=%region_16.17 | all-reduce | flops 2 | bytes 16 | tf_op jit(solution)/shard_map/psum | solution.py:179
  (190 shorter events, 113.9 us)
Async XLA Ops:
  7.2 18.5 %copy-start = (bf16[768,2304]{1,0:T(8,128)(2,1)S(1)}, bf16[768,2304]{1,0:T(8,128)(2,1)}, u32[]{:S(2)}) copy-start(bf16[768,2304]{1,0:T(8,128)(2,1)} %param.20) | copy-start | bytes 10616836
  7.2 48.0 %all-gather.3.cloned.1.call-start = ((), (), s32[]{:S(2)}) async-start(), calls=%async_computation | async-start | bytes 1769472 | tf_op jit(solution)/shard_map/all_gather | solution.py:138
  7.2 16.2 %copy-start.6 = (s32[256]{0:T(256)}, s32[256]{0:T(256)S(1)}, u32[]{:S(2)}) copy-start(s32[256]{0:T(256)S(1)} %and_select_fusion.1) | copy-start | bytes 3076
  14.0 9.5 %copy-start.4 = (f32[768]{0:T(1024)S(1)}, f32[768]{0:T(1024)}, u32[]{:S(2)}) copy-start(f32[768]{0:T(1024)} %param.18) | copy-start | bytes 9220
  14.0 9.5 %copy-start.9 = (s32[1,1,128]{2,1,0:T(1,128)S(1)}, s32[1,1,128]{2,1,0:T(1,128)}, u32[]{:S(2)}) copy-start(s32[1,1,128]{2,1,0:T(1,128)} %param.15) | copy-start | bytes 1540
  14.0 11.7 %copy-start.8 = (f32[768]{0:T(1024)S(1)}, f32[768]{0:T(1024)}, u32[]{:S(2)}) copy-start(f32[768]{0:T(1024)} %param.19) | copy-start | bytes 9220
  24.9 0.8 copy-start.3
  27.2 54.2 %all-gather.5.cloned.1.call-start = ((), (), s32[]{:S(2)}) async-start(), calls=%async_computation.1 | async-start | bytes 1769472 | tf_op jit(solution)/shard_map/all_gather | solution.py:139
  89.0 3.4 %copy-start.1 = (f32[12,128,64]{1,2,0:T(8,128)S(1)}, f32[12,128,64]{1,2,0:T(8,128)}, u32[]{:S(2)}) copy-start(f32[12,128,64]{1,2,0:T(8,128)} %get-tuple-element.187) | copy-start | bytes 1179652 | tf_op jit(solution)/shard_map/while/body/eval_jaxpr/cond
  92.7 0.7 copy-start.2
  97.2 3.3 %copy-start.1 = (f32[12,128,64]{1,2,0:T(8,128)S(1)}, f32[12,128,64]{1,2,0:T(8,128)}, u32[]{:S(2)}) copy-start(f32[12,128,64]{1,2,0:T(8,128)} %get-tuple-element.187) | copy-start | bytes 1179652 | tf_op jit(solution)/shard_map/while/body/eval_jaxpr/cond
  100.9 0.7 copy-start.2
  105.4 3.4 %copy-start.1 = (f32[12,128,64]{1,2,0:T(8,128)S(1)}, f32[12,128,64]{1,2,0:T(8,128)}, u32[]{:S(2)}) copy-start(f32[12,128,64]{1,2,0:T(8,128)} %get-tuple-element.187) | copy-start | bytes 1179652 | tf_op jit(solution)/shard_map/while/body/eval_jaxpr/cond
  109.1 0.7 copy-start.2
  113.5 3.4 %copy-start.1 = (f32[12,128,64]{1,2,0:T(8,128)S(1)}, f32[12,128,64]{1,2,0:T(8,128)}, u32[]{:S(2)}) copy-start(f32[12,128,64]{1,2,0:T(8,128)} %get-tuple-element.187) | copy-start | bytes 1179652 | tf_op jit(solution)/shard_map/while/body/eval_jaxpr/cond
  117.2 0.7 copy-start.2
  121.7 3.3 %copy-start.1 = (f32[12,128,64]{1,2,0:T(8,128)S(1)}, f32[12,128,64]{1,2,0:T(8,128)}, u32[]{:S(2)}) copy-start(f32[12,128,64]{1,2,0:T(8,128)} %get-tuple-element.187) | copy-start | bytes 1179652 | tf_op jit(solution)/shard_map/while/body/eval_jaxpr/cond
  125.4 0.7 copy-start.2
  129.9 3.4 %copy-start.1 = (f32[12,128,64]{1,2,0:T(8,128)S(1)}, f32[12,128,64]{1,2,0:T(8,128)}, u32[]{:S(2)}) copy-start(f32[12,128,64]{1,2,0:T(8,128)} %get-tuple-element.187) | copy-start | bytes 1179652 | tf_op jit(solution)/shard_map/while/body/eval_jaxpr/cond
  133.6 0.7 copy-start.2
  138.1 3.4 %copy-start.1 = (f32[12,128,64]{1,2,0:T(8,128)S(1)}, f32[12,128,64]{1,2,0:T(8,128)}, u32[]{:S(2)}) copy-start(f32[12,128,64]{1,2,0:T(8,128)} %get-tuple-element.187) | copy-start | bytes 1179652 | tf_op jit(solution)/shard_map/while/body/eval_jaxpr/cond
  141.8 0.7 copy-start.2
  146.2 3.3 %copy-start.1 = (f32[12,128,64]{1,2,0:T(8,128)S(1)}, f32[12,128,64]{1,2,0:T(8,128)}, u32[]{:S(2)}) copy-start(f32[12,128,64]{1,2,0:T(8,128)} %get-tuple-element.187) | copy-start | bytes 1179652 | tf_op jit(solution)/shard_map/while/body/eval_jaxpr/cond
  149.9 0.7 copy-start.2
  150.7 5.2 %copy-start.5 = (f32[768]{0:T(1024)S(1)}, f32[768]{0:T(1024)}, u32[]{:S(2)}) copy-start(f32[768]{0:T(1024)} %param.21) | copy-start | bytes 9220
  150.7 6.6 %copy-start.7 = (s32[256]{0:T(256)S(1)}, s32[256]{0:T(256)}, u32[]{:S(2)}) copy-start(s32[256]{0:T(256)} %copy-done.6) | copy-start | bytes 3076
  152.5 4.9 %copy-start.10 = (s32[1,1,128]{2,1,0:T(1,128)S(1)}, s32[1,1,128]{2,1,0:T(1,128)}, u32[]{:S(2)}) copy-start(s32[1,1,128]{2,1,0:T(1,128)} %param.15) | copy-start | bytes 1540
  186.8 59.6 %collective-permute-start.1 = (bf16[4,1,2048]{2,1,0:T(2,128)(2,1)}, bf16[4,1,2048]{2,1,0:T(2,128)(2,1)}, u32[]{:S(2)}, u32[]{:S(2)}) collective-permute-start(bf16[4,1,2048]{2,1,0:T(2,128)(2,1)} %slice.87), channel_id=1, source_target_pairs={{0,24},{8,0},{16,8},{24,16},{1,25},{9,1},{17,9},{25,17},{2,26},{10... | collective-permute-start | bytes 49160 | tf_op jit(solution)/shard_map/ppermute | solution.py:26
  194.1 47.4 %collective-permute-start = (bf16[1,4,2048]{2,1,0:T(4,128)(2,1)}, bf16[1,4,2048]{2,1,0:T(4,128)(2,1)S(1)}, u32[]{:S(2)}, u32[]{:S(2)}) collective-permute-start(bf16[1,4,2048]{2,1,0:T(4,128)(2,1)} %convert_element_type.46), channel_id=1, source_target_pairs={{0,7},{1,0},{2,1},{3,2},{4,3},{5,4},{6,5},{7,6},{8,15},{9,8},{10,9... | collective-permute-start | bytes 49160 | tf_op jit(solution)/shard_map/ppermute | solution.py:26
Sparse Core Ops, SparseCore 0:
  27.3 27.7 all-gather.2
  56.8 24.5 all-gather.4
where the time goes:
time: 314 us; the launch traced here: 311 us
  local copies, waits for them, and re-layouts  142 us (45%)
  waiting for transfers between devices  46.3 us (15%)
  blocking collectives  38.1 us (12%)
  other arithmetic  37.5 us (12%)
  between operations  16.8 us (5%)
  matrix products  16.2 us (5%)
  loops' own time  10.4 us (3%)
  starting transfers between devices  3.97 us (1%)
    psum x1, blocking collectives, shards(): sum_log, sum_act = lax.psum((local_log, local_act), ('space', 'tm'))  38.1 us
    all_gather x1, waiting for transfers between devices, shards(): lax.all_gather(qkv_rows[:, 2 * D:], 'tm', axis=0, tiled=True)  23.7 us
    all_gather x1, waiting for transfers between devices, shards(): lax.all_gather(qkv_rows[:, D:2 * D], 'tm', axis=0, tiled=True)  22 us
    dynamic_slice x16, local copies, waits for them, and re-layouts, fold_rows(): lax.scan(visit_block, carry_in, (jnp.arange(row_total // BLK, dtype=jnp.i...  18.4 us
    concatenate x4, local copies, waits for them, and re-layouts, shards(): next_slab_field = jnp.concatenate([new_field[:, 1:], ahead_slab], axis=1)  15.3 us
    reshape x3, local copies, waits for them, and re-layouts, shards(): next_y_field = jnp.roll(cube, -1, 2).reshape(P_SIZE, P_SIZE, LY * LZ)  11.9 us
    reshape x3, local copies, waits for them, and re-layouts, shards(): next_z_field = jnp.roll(cube, -1, 3).reshape(P_SIZE, P_SIZE, LY * LZ)  11.9 us
    slice x3, local copies, waits for them, and re-layouts, shards(): next_time_field = jnp.concatenate([new_field[1:], ahead_time], axis=0)  11.2 us
  transfers between devices with their start and end apart: 4, of which 2 were waited for; matrix products, arithmetic and copies ran while one was open for 20% of the time, Pallas kernels for 0%

commit v1 on v0

v1 whole, which is shorter than its diff:
```python
import functools
import math

import jax
import jax.numpy as jnp
from jax import lax
from jax.experimental import pallas as pl
from jax.experimental.pallas import tpu as pltpu
from jax.sharding import PartitionSpec as P

D = 768
HS = 64
TOK = 128
PATCH = 256
hopping = 0.2
quartic = 0.5
epsilon = 1e-05
log_two_pi = math.log(2.0 * math.pi)
MESH = pl.DeviceIdType.MESH
f32 = jnp.float32
bf16 = jnp.bfloat16


def iota(shape, dim):
    return lax.broadcasted_iota(jnp.int32, shape, dim)


def dot(a, b):
    return jnp.dot(a, b, preferred_element_type=f32)


def dot_nt(a, b):
    return lax.dot_general(a, b, (((1,), (1,)), ((), ())), preferred_element_type=f32)


def layer_norm(values, gain_vec):
    centre = values - jnp.mean(values, axis=-1, keepdims=True)
    spread = jnp.mean(centre * centre, axis=-1, keepdims=True)
    return centre * lax.rsqrt(spread + epsilon) * gain_vec


def swap_blocks(m, n_out):
    rows = []
    for b in range(8):
        rows.append(
            jnp.concatenate(
                [m[a * 16 : a * 16 + 16, b * 32 : b * 32 + 32] for a in range(8)], axis=1
            )
        )
    return jnp.concatenate(rows, axis=0)


def fold8(a):
    return jnp.sum(a.reshape(a.shape[0] // 8, 8, 128), axis=0)


def kernel(n_s, n_tm, masked, *refs):
    if masked:
        list_ref, refs = refs[0], refs[1:]
    (x_ref, par_ref, we_hbm, be_ref, gi_ref, wq_hbm, go_ref, wh_hbm, bh_ref,
     nf_ref, ad_ref, tl_ref, sl_ref, tot_ref,
     we, wq, wh, wep, whp, a1, a2, b2, tok, emb, nrm, qs, kv, mix,
     ht_s, ht_r, hx_s, hx_r, red_s, red_t,
     w_sem, send, recv, fsend, frecv, sib_sem, halo_sem, rs_send, rs_recv, rt_send, rt_recv) = refs
    n_c = n_tm // 2
    me_t = lax.axis_index("tm")
    me_s = lax.axis_index("space")
    core = lax.rem(me_t, 2)
    chip = me_t // 2
    sibling = chip * 2 + 1 - core

    loads = [
        pltpu.make_async_copy(src, dst, w_sem.at[i])
        for i, (src, dst) in enumerate(((we_hbm, we), (wq_hbm, wq), (wh_hbm, wh)))
    ]
    for load in loads:
        load.start()
    barrier = pltpu.get_barrier_semaphore()
    for o in range(1, n_tm):
        pl.semaphore_signal(barrier, inc=1, device_id={"tm": lax.rem(me_t + o, n_tm)}, device_id_type=MESH)
    for o in range(1, n_s):
        pl.semaphore_signal(barrier, inc=1, device_id={"space": lax.rem(me_s + o, n_s)}, device_id_type=MESH)

    for t in range(4):
        for c in range(16):
            a1[pl.ds(t * 64 + c, 4, stride=16), :] = x_ref[t, :, c * 128 : c * 128 + 128]
    par_row = par_ref[0].astype(f32)
    spread_rows = jnp.where(iota((16, 128), 1) // 16 == iota((16, 128), 0) // 2, par_row, 0.0)
    pick = iota((128, 128), 0) % 16 == (iota((128, 128), 1) % 64) // 4
    par16 = dot(spread_rows.astype(bf16), jnp.where(pick, 1.0, 0.0).astype(bf16))
    par_full = jnp.concatenate([par16] * 16, axis=0)
    row = iota((256, 128), 0)
    lane = iota((256, 128), 1)
    site = (row // 64 + row // 16 + lane // 64 + lane) % 2
    frozen = site.astype(f32) == par_full
    u = a1[...]
    a2[...] = jnp.where(frozen, u, 0.0)
    rows_c = jnp.concatenate([a2[pl.ds(c, 16, stride=16), :] for c in range(16)], axis=0)
    r, l = iota((128, 128), 0), iota((128, 128), 1)
    q = jnp.where((r // 64 == l // 64) & ((r % 64) // 16 == l % 4) & (r % 16 == (l % 64) // 4), 1.0, 0.0).astype(bf16)
    spreadq = dot_nt(q, rows_c.astype(bf16))
    tok[me_t] = swap_blocks(spreadq, 8).astype(bf16)

    pl.semaphore_wait(barrier, n_tm - 1 + n_s - 1)
    own = pltpu.make_async_remote_copy(
        src_ref=tok.at[me_t], dst_ref=tok.at[me_t], send_sem=sib_sem.at[0], recv_sem=sib_sem.at[1],
        device_id={"tm": sibling}, device_id_type=MESH)
    sends = []
    for k in range(1, n_c):
        target = lax.rem(chip + k, n_c) * 2 + core
        sends.append(pltpu.make_async_remote_copy(
            src_ref=tok.at[me_t], dst_ref=tok.at[me_t], send_sem=send.at[k - 1], recv_sem=recv.at[k - 1],
            device_id={"tm": target}, device_id_type=MESH))
    for s in sends:
        s.start()
    own.start()
    forwards = []
    for k in range(1, n_c):
        block = lax.rem(chip - k + n_c, n_c) * 2 + core
        forwards.append(pltpu.make_async_remote_copy(
            src_ref=tok.at[block], dst_ref=tok.at[block], send_sem=fsend.at[k - 1], recv_sem=frecv.at[k - 1],
            device_id={"tm": sibling}, device_id_type=MESH))

    f, j = iota((256, 256), 0), iota((256, 256), 1)
    d = f // 32
    source = (f % 16) * 16 + ((f // 16) % 2) * 8 + (d // 4) * 4 + d % 4
    perm = jnp.where(j == source, 1.0, 0.0).astype(bf16)
    loads[0].wait()
    wep[...] = dot(perm, we[...]).astype(bf16)
    loads[2].wait()
    whp[:, :256] = dot_nt(wh[:, :256], perm).astype(bf16)
    whp[:, 256:] = dot_nt(wh[:, 256:], perm).astype(bf16)
    b_head = bh_ref[...].reshape(2, 256)
    b_hi = b_head.astype(bf16).astype(f32)
    b_mid = (b_head - b_hi).astype(bf16).astype(f32)
    b_lo = b_head - b_hi - b_mid
    parts = jnp.concatenate([b_hi, b_mid, b_lo, jnp.zeros((2, 256), f32)], axis=0)
    moved_b = dot_nt(parts.astype(bf16), perm)
    b_perm = moved_b[0:2] + moved_b[2:4] + moved_b[4:6]
    b_embed = be_ref[...].reshape(1, D)
    gain_in = gi_ref[...].reshape(1, D)
    loads[1].wait()

    for k in range(n_c):
        here = lax.rem(chip - k + n_c, n_c)
        if k == 0:
            own.wait_recv()
        else:
            if k == 1:
                sends[0].wait_recv()
                forwards[0].start()
            if k < n_c - 1:
                sends[k].wait_recv()
                forwards[k].start()
            forwards[k - 1].wait_recv()
        pair = tok[pl.ds(here * 2, 2)].reshape(2 * TOK, PATCH)
        embedded = dot(pair, wep[...]) + b_embed
        normed = layer_norm(embedded, gain_in).astype(bf16)
        if k == 0:
            emb[...] = embedded
            nrm[...] = normed
            mine = pl.ds(pl.multiple_of(core * TOK, TOK), TOK)
            qs[...] = dot(nrm[mine, :], wq[:, :D]).astype(bf16) * jnp.asarray(HS ** (-0.5), bf16)
        rows_at = pl.ds(pl.multiple_of(here * 2 * TOK, 2 * TOK), 2 * TOK)
        kv[rows_at, :] = dot(normed, wq[:, D:]).astype(bf16)

    if masked:
        nb, ksel = list_ref.shape
        mine_row = jnp.sum(jnp.where(iota((nb, ksel), 0) == me_t, list_ref[...], 0), axis=0, keepdims=True)
        key_block = iota((1, n_tm * TOK), 1) // TOK
        listed = key_block < 0
        for i in range(ksel):
            listed = listed | (key_block == mine_row[:, i : i + 1])
        bias = jnp.where(listed, 0.0, -1e30)
    low = iota((TOK, 128), 1) < HS

    def head_pair(h, carry):
        cols = pl.ds(pl.multiple_of(h * 128, 128), 128)
        vcols = pl.ds(pl.multiple_of(D + h * 128, 128), 128)
        qq = qs[:, cols]
        zero = jnp.zeros_like(qq)
        q2 = jnp.concatenate([jnp.where(low, qq, zero), jnp.where(low, zero, qq)], axis=0)
        s = dot_nt(q2, kv[:, cols])
        if masked:
            s = s + bias
        top = jnp.max(s, axis=-1, keepdims=True)
        ex = jnp.exp(s - top)
        total = jnp.sum(ex, axis=-1, keepdims=True)
        o = dot(ex.astype(bf16), kv[:, vcols]) / total
        mix[:, cols] = jnp.where(low, o[:TOK], o[TOK:])
        return carry

    lax.fori_loop(0, D // 128, head_pair, 0)

    hidden = emb[mine, :] + mix[...]
    normed_out = layer_norm(hidden, go_ref[...].reshape(1, D)).astype(bf16)
    raw = dot(normed_out, whp[...])
    scale_tok = jnp.tanh(raw[:, :256] + b_perm[0:1])
    shift_tok = raw[:, 256:] + b_perm[1:2]

    def to_lattice(values, ref):
        flipped = jnp.transpose(swap_blocks(values, 8))
        hi = flipped.astype(bf16)
        lo = (flipped - hi.astype(f32)).astype(bf16)
        ref[...] = dot(hi, q) + dot(lo, q)
        return jnp.concatenate([ref[pl.ds(i, 16, stride=16), :] for i in range(16)], axis=0)

    scale_log = to_lattice(scale_tok, a2)
    shift_val = to_lattice(shift_tok, b2)
    field = jnp.where(frozen, u, u * jnp.exp(scale_log) + shift_val)
    ht_s[...] = field[0:64].astype(bf16)
    hx_s[...] = jnp.concatenate([field[t * 64 : t * 64 + 16] for t in range(4)], axis=0).astype(bf16)
    halo_t = pltpu.make_async_remote_copy(
        src_ref=ht_s, dst_ref=ht_r, send_sem=halo_sem.at[0], recv_sem=halo_sem.at[1],
        device_id={"tm": lax.rem(me_t - 1 + n_tm, n_tm)}, device_id_type=MESH)
    halo_x = pltpu.make_async_remote_copy(
        src_ref=hx_s, dst_ref=hx_r, send_sem=halo_sem.at[2], recv_sem=halo_sem.at[3],
        device_id={"space": lax.rem(me_s - 1 + n_s, n_s)}, device_id_type=MESH)
    halo_t.start()
    halo_x.start()

    def put(ref, out):
        for t in range(4):
            for c in range(16):
                out[t, :, c * 128 : c * 128 + 128] = ref[pl.ds(t * 64 + c, 4, stride=16), :]

    a1[...] = field
    put(a1, nf_ref)
    log_part = -0.5 * fold8(u * u) - fold8(jnp.where(frozen, 0.0, scale_log))
    ahead = pltpu.roll(field, 127, 1)
    wrapped = pltpu.roll(field, 63, 1)
    next_z = jnp.where(lane % 64 == 63, wrapped, ahead)
    half = pltpu.roll(field, 64, 1)
    up = pltpu.roll(half, 255, 0)
    up_wrap = pltpu.roll(half, 15, 0)
    next_y = jnp.where(lane < 64, half, jnp.where(row % 16 == 15, up_wrap, up))
    halo_t.wait_recv()
    next_t = jnp.concatenate([field[64:], ht_r[...].astype(f32)], axis=0)
    halo_x.wait_recv()
    hx = hx_r[...].astype(f32)
    pieces = []
    for t in range(4):
        pieces += [field[t * 64 + 16 : t * 64 + 64], hx[t * 16 : t * 16 + 16]]
    next_x = jnp.concatenate(pieces, axis=0)
    neighbours = next_t + next_x
    neighbours = neighbours + next_y
    neighbours = neighbours + next_z
    squared = field * field
    density = -2.0 * hopping * field * neighbours + squared + quartic * (squared - 1.0) * (squared - 1.0)

    red_s[me_s] = jnp.concatenate([log_part, fold8(density)], axis=0)
    s_sends = [
        pltpu.make_async_remote_copy(
            src_ref=red_s.at[me_s], dst_ref=red_s.at[me_s], send_sem=rs_send.at[o - 1], recv_sem=rs_recv.at[o - 1],
            device_id={"space": lax.rem(me_s + o, n_s)}, device_id_type=MESH)
        for o in range(1, n_s)
    ]
    for s in s_sends:
        s.start()
    a1[...] = density
    put(a1, ad_ref)
    a2[...] = field * next_t
    put(a2, tl_ref)
    for s in s_sends:
        s.wait_recv()
    red_t[me_t] = jnp.sum(red_s[...], axis=0)
    t_sends = [
        pltpu.make_async_remote_copy(
            src_ref=red_t.at[me_t], dst_ref=red_t.at[me_t], send_sem=rt_send.at[o - 1], recv_sem=rt_recv.at[o - 1],
            device_id={"tm": lax.rem(me_t + o, n_tm)}, device_id_type=MESH)
        for o in range(1, n_tm)
    ]
    for s in t_sends:
        s.start()
    b2[...] = field * next_x
    put(b2, sl_ref)
    own.wait_send()
    for s in sends + forwards:
        s.wait_send()
    halo_t.wait_send()
    halo_x.wait_send()
    for s in s_sends:
        s.wait_send()
    for s in t_sends:
        s.wait_recv()
    whole = jnp.sum(red_t[...], axis=0)
    sites = n_s * n_tm * 256 * 128
    tot_ref[0] = jnp.sum(whole[0:8]) / sites - 0.5 * log_two_pi
    tot_ref[1] = jnp.sum(whole[8:16]) / sites
    for s in t_sends:
        s.wait_send()


def shards(n_s, n_tm, lattice_field, parity, block_list, *weights):
    masked = block_list.shape[0] != block_list.shape[1]
    vm = pl.BlockSpec(memory_space=pltpu.VMEM)
    hbm = pl.BlockSpec(memory_space=pl.ANY)
    n_c = n_tm // 2
    grid_shape = jax.ShapeDtypeStruct(lattice_field.shape, f32)
    dma = pltpu.SemaphoreType.DMA
    call = pl.pallas_call(
        functools.partial(kernel, n_s, n_tm, masked),
        out_shape=(grid_shape,) * 4 + (jax.ShapeDtypeStruct((2,), f32),),
        in_specs=([vm] if masked else []) + [vm, vm, hbm, vm, vm, hbm, vm, hbm, vm],
        out_specs=(vm,) * 4 + (pl.BlockSpec(memory_space=pltpu.SMEM),),
        scratch_shapes=[
            pltpu.VMEM((PATCH, D), bf16),
            pltpu.VMEM((D, 3 * D), bf16),
            pltpu.VMEM((D, 2 * PATCH), bf16),
            pltpu.VMEM((PATCH, D), bf16),
            pltpu.VMEM((D, 2 * PATCH), bf16),
            pltpu.VMEM((256, 128), f32),
            pltpu.VMEM((256, 128), f32),
            pltpu.VMEM((256, 128), f32),
            pltpu.VMEM((n_tm, TOK, PATCH), bf16),
            pltpu.VMEM((2 * TOK, D), f32),
            pltpu.VMEM((2 * TOK, D), bf16),
            pltpu.VMEM((TOK, D), bf16),
            pltpu.VMEM((n_tm * TOK, 2 * D), bf16),
            pltpu.VMEM((TOK, D), f32),
            pltpu.VMEM((64, 128), bf16),
            pltpu.VMEM((64, 128), bf16),
            pltpu.VMEM((64, 128), bf16),
            pltpu.VMEM((64, 128), bf16),
            pltpu.VMEM((n_s, 16, 128), f32),
            pltpu.VMEM((n_tm, 16, 128), f32),
            dma((3,)),
            dma((n_c - 1,)),
            dma((n_c - 1,)),
            dma((n_c - 1,)),
            dma((n_c - 1,)),
            dma((2,)),
            dma((4,)),
            dma((n_s - 1,)),
            dma((n_s - 1,)),
            dma((n_tm - 1,)),
            dma((n_tm - 1,)),
        ],
        compiler_params=pltpu.CompilerParams(
            collective_id=0, has_side_effects=True, vmem_limit_bytes=40 * 2**20
        ),
        cost_estimate=pl.CostEstimate(flops=5 * 10**9, bytes_accessed=6 * 10**6, transcendentals=2 * 10**6),
    )
    extra = (block_list,) if masked else ()
    return call(*extra, lattice_field, parity, *weights)


def solution(mesh):
    n_s, n_tm = mesh.shape["space"], mesh.shape["tm"]
    split = P("tm", "space", None)
    return jax.shard_map(
        functools.partial(shards, n_s, n_tm),
        mesh=mesh,
        in_specs=(split, split) + (P(),) * 8,
        out_specs=(split,) * 4 + (P(),),
        check_vma=False,
    )
```

time: 314 us -> 45.8 us (0.15)
  local copies, waits for them, and re-layouts: 142 us -> 11.6 us
  waiting for transfers between devices: 46.3 us -> 0 us
  blocking collectives: 38.1 us -> 0 us
  other arithmetic: 37.5 us -> 0 us
  Pallas kernels: 0 us -> 33.2 us
  matrix products: 16.2 us -> 0 us
  between operations: 16.8 us -> 0.66 us
  loops' own time: 10.4 us -> 0 us
  starting transfers between devices: 3.97 us -> 0 us
    all_gather x2 -> x0, waiting for transfers between devices: 45.6 us -> none  [the longest x1 23.7 us: shards(): lax.all_gather(qkv_rows[:, 2 * D:], 'tm', axis=0, tiled=True)]
    reshape x12 -> x0, local copies, waits for them, and re-layouts: 44 us -> none  [the longest x3 11.9 us: shards(): next_y_field = jnp.roll(cube, -1, 2).reshape(P_SIZE, P_SIZE, LY * LZ)]
    psum x1 -> x0, blocking collectives: 38.1 us -> none  [shards(): sum_log, sum_act = lax.psum((local_log, local_act), ('space', 'tm'))]
    pallas_call x0 -> x1, Pallas kernels: none -> 33.2 us  [shards(): return call(*extra, lattice_field, parity, *weights)]
    slice x11 -> x0, local copies, waits for them, and re-layouts: 24.2 us -> none  [the longest x3 11.2 us: shards(): next_time_field = jnp.concatenate([new_field[1:], ahead_time], axis=0)]
    concatenate x6 -> x0, local copies, waits for them, and re-layouts: 20.2 us -> none  [the longest x4 15.3 us: shards(): next_slab_field = jnp.concatenate([new_field[:, 1:], ahead_slab], axis=1)]
    dynamic_slice x17 -> x0, local copies, waits for them, and re-layouts: 19.6 us -> none  [the longest x16 18.4 us: fold_rows(): lax.scan(visit_block, carry_in, (jnp.arange(row_total // BLK, dtype=jnp.i...]
    reduce_or x16 -> x0, other arithmetic: 16.4 us -> none  [the longest x8 10.1 us: visit_block(): needed = jnp.any(block_rows == block_id)]
  transfers between devices with their start and end apart: 4 -> 0, of which waited for: 2 -> 0; matrix products, arithmetic and copies ran while one was open for 20% -> 0% of each run, Pallas kernels for 0% -> 0%
where the time goes in v1:
time: 45.8 us; the launch traced here: 45.4 us
  Pallas kernels  33.2 us (72%)
  local copies, waits for them, and re-layouts  11.6 us (25%)
  between operations  0.66 us (1%)
    pallas_call x1, Pallas kernels, shards(): return call(*extra, lattice_field, parity, *weights)  33.2 us
    unnamed x23, local copies, waits for them, and re-layouts  11.6 us

profile of v1, /device:TPU:0, one launch (start us, length us, event | category | flops | bytes accessed | tf_op | source)
XLA Modules:
  0.0 45.4 jit_solution(7820108543433700729)
XLA Ops:
  0.6 0.0 copy-start
  0.6 2.0 %copy-done = bf16[768,2304]{1,0:T(8,128)(2,1)S(1)} copy-done((bf16[768,2304]{1,0:T(8,128)(2,1)S(1)}, bf16[768,2304]{1,0:T(8,128)(2,1)}, u32[]{:S(2)}) %copy-start) | copy-done | bytes 3538968
  2.6 0.0 copy-start.1
  2.6 1.1 %copy-done.1 = bf16[768,512]{1,0:T(8,128)(2,1)S(1)} copy-done((bf16[768,512]{1,0:T(8,128)(2,1)S(1)}, bf16[768,512]{1,0:T(8,128)(2,1)}, u32[]{:S(2)}) %copy-start.1) | copy-done | bytes 786456
  3.8 0.0 copy-start.2
  3.8 1.0 %copy-done.2 = bf16[256,768]{1,0:T(8,128)(2,1)S(1)} copy-done((bf16[256,768]{1,0:T(8,128)(2,1)S(1)}, bf16[256,768]{1,0:T(8,128)(2,1)}, u32[]{:S(2)}) %copy-start.2) | copy-done | bytes 393240
  4.8 0.0 copy-start.3
  4.8 0.9 %copy-done.3 = f32[4,4,2048]{2,1,0:T(4,128)S(1)} copy-done((f32[4,4,2048]{2,1,0:T(4,128)S(1)}, f32[4,4,2048]{2,1,0:T(4,128)}, u32[]{:S(2)}) %copy-start.3) | copy-done | bytes 131096
  5.7 0.0 copy-start.4
  5.7 0.7 %copy-done.4 = f32[768]{0:T(1024)S(1)} copy-done((f32[768]{0:T(1024)S(1)}, f32[768]{0:T(1024)}, u32[]{:S(2)}) %copy-start.4) | copy-done | bytes 3096
  6.4 0.0 copy-start.5
  6.4 0.7 %copy-done.5 = f32[768]{0:T(1024)S(1)} copy-done((f32[768]{0:T(1024)S(1)}, f32[768]{0:T(1024)}, u32[]{:S(2)}) %copy-start.5) | copy-done | bytes 3096
  7.0 0.0 copy-start.6
  7.0 0.7 %copy-done.6 = f32[768]{0:T(1024)S(1)} copy-done((f32[768]{0:T(1024)S(1)}, f32[768]{0:T(1024)}, u32[]{:S(2)}) %copy-start.6) | copy-done | bytes 3096
  7.7 0.0 copy-start.7
  7.7 0.7 %copy-done.7 = f32[512]{0:T(512)S(1)} copy-done((f32[512]{0:T(512)S(1)}, f32[512]{0:T(512)}, u32[]{:S(2)}) %copy-start.7) | copy-done | bytes 2072
  8.4 0.0 copy-start.8
  8.4 0.7 %copy-done.8 = s32[1,1,128]{2,1,0:T(1,128)S(1)} copy-done((s32[1,1,128]{2,1,0:T(1,128)S(1)}, s32[1,1,128]{2,1,0:T(1,128)}, u32[]{:S(2)}) %copy-start.8) | copy-done | bytes 536
  9.1 33.2 %shard_map.128 = (f32[4,4,2048]{2,1,0:T(4,128)S(1)}, f32[4,4,2048]{2,1,0:T(4,128)S(1)}, f32[4,4,2048]{2,1,0:T(4,128)S(1)}, f32[4,4,2048]{2,1,0:T(4,128)S(1)}, f32[2]{0:T(128)S(1)}) custom-call(f32[4,4,2048]{2,1,0:T(4,128)S(1)} %copy-done.3, s32[1,1,128]{2,1,0:T(1,128)S(1)} %copy-done.8, bf16[256,768]{1,0:T(8,128)(2,1)S(1)} %copy-done.2, f32[768]{0:T(1024)S(1)} %copy-done.4, ...), custom_call_target="tpu_custom_call" | custom-call | flops 5000000000 | bytes 6000000 | tf_op jit(solution)/shard_map/pallas_call | solution.py:345
  42.3 0.7 %copy.19 = f32[4,4,2048]{2,1,0:T(4,128)} copy(f32[4,4,2048]{2,1,0:T(4,128)S(1)} %get-tuple-element.10) | data formatting | bytes 262144
  42.9 0.7 %copy.20 = f32[4,4,2048]{2,1,0:T(4,128)} copy(f32[4,4,2048]{2,1,0:T(4,128)S(1)} %get-tuple-element.11) | data formatting | bytes 262144
  43.6 0.7 %copy.21 = f32[4,4,2048]{2,1,0:T(4,128)} copy(f32[4,4,2048]{2,1,0:T(4,128)S(1)} %get-tuple-element.12) | data formatting | bytes 262144
  44.2 0.7 %copy.22 = f32[4,4,2048]{2,1,0:T(4,128)} copy(f32[4,4,2048]{2,1,0:T(4,128)S(1)} %get-tuple-element.13) | data formatting | bytes 262144
  44.9 0.5 %copy.23 = f32[2]{0:T(128)} copy(f32[2]{0:T(128)S(1)} %get-tuple-element.14) | data formatting | bytes 16
Async XLA Ops:
  0.6 2.0 %copy-start = (bf16[768,2304]{1,0:T(8,128)(2,1)S(1)}, bf16[768,2304]{1,0:T(8,128)(2,1)}, u32[]{:S(2)}) copy-start(bf16[768,2304]{1,0:T(8,128)(2,1)} %refs_5_.1) | copy-start | bytes 10616836
  2.6 1.1 %copy-start.1 = (bf16[768,512]{1,0:T(8,128)(2,1)S(1)}, bf16[768,512]{1,0:T(8,128)(2,1)}, u32[]{:S(2)}) copy-start(bf16[768,512]{1,0:T(8,128)(2,1)} %refs_7_.1) | copy-start | bytes 2359300
  3.8 1.0 %copy-start.2 = (bf16[256,768]{1,0:T(8,128)(2,1)S(1)}, bf16[256,768]{1,0:T(8,128)(2,1)}, u32[]{:S(2)}) copy-start(bf16[256,768]{1,0:T(8,128)(2,1)} %refs_2_.1) | copy-start | bytes 1179652
  4.8 0.9 %copy-start.3 = (f32[4,4,2048]{2,1,0:T(4,128)S(1)}, f32[4,4,2048]{2,1,0:T(4,128)}, u32[]{:S(2)}) copy-start(f32[4,4,2048]{2,1,0:T(4,128)} %refs_0_.1) | copy-start | bytes 393220
  5.7 0.7 %copy-start.4 = (f32[768]{0:T(1024)S(1)}, f32[768]{0:T(1024)}, u32[]{:S(2)}) copy-start(f32[768]{0:T(1024)} %refs_3_.1) | copy-start | bytes 9220
  6.4 0.7 %copy-start.5 = (f32[768]{0:T(1024)S(1)}, f32[768]{0:T(1024)}, u32[]{:S(2)}) copy-start(f32[768]{0:T(1024)} %refs_4_.1) | copy-start | bytes 9220
  7.0 0.7 %copy-start.6 = (f32[768]{0:T(1024)S(1)}, f32[768]{0:T(1024)}, u32[]{:S(2)}) copy-start(f32[768]{0:T(1024)} %refs_6_.1) | copy-start | bytes 9220
  7.7 0.7 %copy-start.7 = (f32[512]{0:T(512)S(1)}, f32[512]{0:T(512)}, u32[]{:S(2)}) copy-start(f32[512]{0:T(512)} %refs_8_.1) | copy-start | bytes 6148
  8.4 0.7 %copy-start.8 = (s32[1,1,128]{2,1,0:T(1,128)S(1)}, s32[1,1,128]{2,1,0:T(1,128)}, u32[]{:S(2)}) copy-start(s32[1,1,128]{2,1,0:T(1,128)} %refs_1_.1) | copy-start | bytes 1540

commit v2 on v1

--- a/solution.py
+++ b/solution.py
@@ -57,11 +57,11 @@
 def kernel(n_s, n_tm, masked, *refs):
     if masked:
         list_ref, refs = refs[0], refs[1:]
-    (x_ref, par_ref, we_hbm, be_ref, gi_ref, wq_hbm, go_ref, wh_hbm, bh_ref,
-     nf_ref, ad_ref, tl_ref, sl_ref, tot_ref,
-     we, wq, wh, wep, whp, a1, a2, b2, tok, emb, nrm, qs, kv, mix,
+    (x_hbm, par_hbm, we_hbm, be_hbm, gi_hbm, wq_hbm, go_hbm, wh_hbm, bh_hbm,
+     nf_hbm, ad_hbm, tl_hbm, sl_hbm, tot_ref, nf_ref, ad_ref, tl_ref, sl_ref,
+     x_ref, par_ref, be_ref, gi_ref, go_ref, bh_ref, we, wq, wh, wep, whp, a1, a2, b2, tok, emb, nrm, qs, kv, mix,
      ht_s, ht_r, hx_s, hx_r, red_s, red_t,
-     w_sem, send, recv, fsend, frecv, sib_sem, halo_sem, rs_send, rs_recv, rt_send, rt_recv) = refs
+     w_sem, o_sem, send, recv, fsend, frecv, sib_sem, halo_sem, rs_send, rs_recv, rt_send, rt_recv) = refs
     n_c = n_tm // 2
     me_t = lax.axis_index("tm")
     me_s = lax.axis_index("space")
@@ -71,7 +71,9 @@
 
     loads = [
         pltpu.make_async_copy(src, dst, w_sem.at[i])
-        for i, (src, dst) in enumerate(((we_hbm, we), (wq_hbm, wq), (wh_hbm, wh)))
+        for i, (src, dst) in enumerate((
+            (x_hbm, x_ref), (par_hbm, par_ref), (we_hbm, we), (wh_hbm, wh), (bh_hbm, bh_ref), (be_hbm, be_ref),
+            (gi_hbm, gi_ref), (wq_hbm, wq), (go_hbm, go_ref)))
     ]
     for load in loads:
         load.start()
@@ -81,6 +83,8 @@
     for o in range(1, n_s):
         pl.semaphore_signal(barrier, inc=1, device_id={"space": lax.rem(me_s + o, n_s)}, device_id_type=MESH)
 
+    loads[0].wait()
+    loads[1].wait()
     for t in range(4):
         for c in range(16):
             a1[pl.ds(t * 64 + c, 4, stride=16), :] = x_ref[t, :, c * 128 : c * 128 + 128]
@@ -125,11 +129,12 @@
     d = f // 32
     source = (f % 16) * 16 + ((f // 16) % 2) * 8 + (d // 4) * 4 + d % 4
     perm = jnp.where(j == source, 1.0, 0.0).astype(bf16)
-    loads[0].wait()
+    loads[2].wait()
     wep[...] = dot(perm, we[...]).astype(bf16)
-    loads[2].wait()
+    loads[3].wait()
     whp[:, :256] = dot_nt(wh[:, :256], perm).astype(bf16)
     whp[:, 256:] = dot_nt(wh[:, 256:], perm).astype(bf16)
+    loads[4].wait()
     b_head = bh_ref[...].reshape(2, 256)
     b_hi = b_head.astype(bf16).astype(f32)
     b_mid = (b_head - b_hi).astype(bf16).astype(f32)
@@ -137,9 +142,12 @@
     parts = jnp.concatenate([b_hi, b_mid, b_lo, jnp.zeros((2, 256), f32)], axis=0)
     moved_b = dot_nt(parts.astype(bf16), perm)
     b_perm = moved_b[0:2] + moved_b[2:4] + moved_b[4:6]
+    loads[5].wait()
+    loads[6].wait()
     b_embed = be_ref[...].reshape(1, D)
     gain_in = gi_ref[...].reshape(1, D)
-    loads[1].wait()
+    loads[7].wait()
+    loads[8].wait()
 
     for k in range(n_c):
         here = lax.rem(chip - k + n_c, n_c)
@@ -190,7 +198,7 @@
         mix[:, cols] = jnp.where(low, o[:TOK], o[TOK:])
         return carry
 
-    lax.fori_loop(0, D // 128, head_pair, 0)
+    lax.fori_loop(0, D // 128, head_pair, 0, unroll=True)
 
     hidden = emb[mine, :] + mix[...]
     normed_out = layer_norm(hidden, go_ref[...].reshape(1, D)).astype(bf16)
@@ -219,13 +227,18 @@
     halo_t.start()
     halo_x.start()
 
-    def put(ref, out):
+    stores = []
+
+    def put(ref, out, hbm):
         for t in range(4):
             for c in range(16):
                 out[t, :, c * 128 : c * 128 + 128] = ref[pl.ds(t * 64 + c, 4, stride=16), :]
+        store = pltpu.make_async_copy(out, hbm, o_sem.at[len(stores)])
+        store.start()
+        stores.append(store)
 
     a1[...] = field
-    put(a1, nf_ref)
+    put(a1, nf_ref, nf_hbm)
     log_part = -0.5 * fold8(u * u) - fold8(jnp.where(frozen, 0.0, scale_log))
     ahead = pltpu.roll(field, 127, 1)
     wrapped = pltpu.roll(field, 63, 1)
@@ -258,9 +271,9 @@
     for s in s_sends:
         s.start()
     a1[...] = density
-    put(a1, ad_ref)
+    put(a1, ad_ref, ad_hbm)
     a2[...] = field * next_t
-    put(a2, tl_ref)
+    put(a2, tl_ref, tl_hbm)
     for s in s_sends:
         s.wait_recv()
     red_t[me_t] = jnp.sum(red_s[...], axis=0)
@@ -273,7 +286,7 @@
     for s in t_sends:
         s.start()
     b2[...] = field * next_x
-    put(b2, sl_ref)
+    put(b2, sl_ref, sl_hbm)
     own.wait_send()
     for s in sends + forwards:
         s.wait_send()
@@ -289,21 +302,42 @@
     tot_ref[1] = jnp.sum(whole[8:16]) / sites
     for s in t_sends:
         s.wait_send()
+    for s in stores:
+        s.wait()
+
+
+def write_out(*refs):
+    sources, targets, sem = refs[:5], refs[5:10], refs[10]
+    copies = [pltpu.make_async_copy(a, b, sem.at[i]) for i, (a, b) in enumerate(zip(sources, targets))]
+    for c in copies:
+        c.start()
+    for c in copies:
+        c.wait()
 
 
 def shards(n_s, n_tm, lattice_field, parity, block_list, *weights):
     masked = block_list.shape[0] != block_list.shape[1]
     vm = pl.BlockSpec(memory_space=pltpu.VMEM)
-    hbm = pl.BlockSpec(memory_space=pl.ANY)
+    hbm = pl.BlockSpec(memory_space=pltpu.HBM)
     n_c = n_tm // 2
     grid_shape = jax.ShapeDtypeStruct(lattice_field.shape, f32)
     dma = pltpu.SemaphoreType.DMA
     call = pl.pallas_call(
         functools.partial(kernel, n_s, n_tm, masked),
         out_shape=(grid_shape,) * 4 + (jax.ShapeDtypeStruct((2,), f32),),
-        in_specs=([vm] if masked else []) + [vm, vm, hbm, vm, vm, hbm, vm, hbm, vm],
-        out_specs=(vm,) * 4 + (pl.BlockSpec(memory_space=pltpu.SMEM),),
+        in_specs=([vm] if masked else []) + [hbm] * 9,
+        out_specs=(hbm,) * 4 + (pl.BlockSpec(memory_space=pltpu.SMEM),),
         scratch_shapes=[
+            pltpu.VMEM(lattice_field.shape, f32),
+            pltpu.VMEM(lattice_field.shape, f32),
+            pltpu.VMEM(lattice_field.shape, f32),
+            pltpu.VMEM(lattice_field.shape, f32),
+            pltpu.VMEM(lattice_field.shape, f32),
+            pltpu.VMEM(parity.shape, jnp.int32),
+            pltpu.VMEM((D,), f32),
+            pltpu.VMEM((D,), f32),
+            pltpu.VMEM((D,), f32),
+            pltpu.VMEM((2 * PATCH,), f32),
             pltpu.VMEM((PATCH, D), bf16),
             pltpu.VMEM((D, 3 * D), bf16),
             pltpu.VMEM((D, 2 * PATCH), bf16),
@@ -324,7 +358,8 @@
             pltpu.VMEM((64, 128), bf16),
             pltpu.VMEM((n_s, 16, 128), f32),
             pltpu.VMEM((n_tm, 16, 128), f32),
-            dma((3,)),
+            dma((9,)),
+            dma((4,)),
             dma((n_c - 1,)),
             dma((n_c - 1,)),
             dma((n_c - 1,)),
@@ -337,12 +372,21 @@
             dma((n_tm - 1,)),
         ],
         compiler_params=pltpu.CompilerParams(
-            collective_id=0, has_side_effects=True, vmem_limit_bytes=40 * 2**20
+            collective_id=0, has_side_effects=True, vmem_limit_bytes=63 * 2**20
         ),
         cost_estimate=pl.CostEstimate(flops=5 * 10**9, bytes_accessed=6 * 10**6, transcendentals=2 * 10**6),
     )
     extra = (block_list,) if masked else ()
-    return call(*extra, lattice_field, parity, *weights)
+    results = call(*extra, lattice_field, parity, *weights)
+    return pl.pallas_call(
+        write_out,
+        out_shape=[jax.ShapeDtypeStruct(r.shape, r.dtype) for r in results],
+        in_specs=[vm] * 5,
+        out_specs=[hbm] * 5,
+        scratch_shapes=[dma((5,))],
+        compiler_params=pltpu.CompilerParams(vmem_limit_bytes=63 * 2**20),
+        cost_estimate=pl.CostEstimate(flops=0, bytes_accessed=2**20, transcendentals=0),
+    )(*results)
 
 
 def solution(mesh):

time: 45.8 us -> 34.2 us (0.75)
  local copies, waits for them, and re-layouts: 11.6 us -> 0 us
    unnamed x23 -> x0, local copies, waits for them, and re-layouts: 11.6 us -> none
    pallas_call x1 -> x2, Pallas kernels: 33.2 us -> 33.4 us  [the longest x1 31.5 us: shards(): results = call(*extra, lattice_field, parity, *weights)]
where the time goes in v2:
time: 34.2 us; the launch traced here: 34 us
  Pallas kernels  33.4 us (98%)
  between operations  0.64 us (2%)
    pallas_call x1, Pallas kernels, shards(): results = call(*extra, lattice_field, parity, *weights)  31.5 us
    pallas_call x1, Pallas kernels, shards(): pl.pallas_call(write_out, out_shape=[jax.ShapeDtypeStruct(r.shape, r.dtyp...  1.93 us

profile of v2, /device:TPU:0, one launch (start us, length us, event | category | flops | bytes accessed | tf_op | source)
XLA Modules:
  0.0 34.0 jit_solution(70436306255654028)
XLA Ops:
  0.6 31.5 %shard_map.128 = (f32[4,4,2048]{2,1,0:T(4,128)}, f32[4,4,2048]{2,1,0:T(4,128)}, f32[4,4,2048]{2,1,0:T(4,128)}, f32[4,4,2048]{2,1,0:T(4,128)}, f32[2]{0:T(128)}) custom-call(f32[4,4,2048]{2,1,0:T(4,128)} %refs_0_.1, s32[1,1,128]{2,1,0:T(1,128)} %refs_1_.1, bf16[256,768]{1,0:T(8,128)(2,1)} %refs_2_.1, f32[768]{0:T(1024)} %refs_3_.1, f32[768]{0:T(1024)} %refs_4_.1, ...), custom_call_target="tpu_custom_call" | custom-call | flops 5000000000 | bytes 6000000 | tf_op jit(solution)/shard_map/pallas_call | solution.py:380
  32.1 1.9 %shard_map.129 = (f32[4,4,2048]{2,1,0:T(4,128)}, f32[4,4,2048]{2,1,0:T(4,128)}, f32[4,4,2048]{2,1,0:T(4,128)}, f32[4,4,2048]{2,1,0:T(4,128)}, f32[2]{0:T(128)}) custom-call(f32[4,4,2048]{2,1,0:T(4,128)} %get-tuple-element.10.refs_0_, f32[4,4,2048]{2,1,0:T(4,128)} %get-tuple-element.11.refs_1_, f32[4,4,2048]{2,1,0:T(4,128)} %get-tuple-element.12.refs_2_, ...), custom_call_target="tpu_custom_call" | custom-call | bytes 1048576 | tf_op jit(solution)/shard_map/pallas_call | solution.py:381

commit v3 on v2

--- a/solution.py
+++ b/solution.py
@@ -39,12 +39,12 @@
     return centre * lax.rsqrt(spread + epsilon) * gain_vec
 
 
-def swap_blocks(m, n_out):
+def swap_blocks(m, n_a, n_b):
     rows = []
-    for b in range(8):
+    for b in range(n_b):
         rows.append(
             jnp.concatenate(
-                [m[a * 16 : a * 16 + 16, b * 32 : b * 32 + 32] for a in range(8)], axis=1
+                [m[a * 16 : a * 16 + 16, b * 32 : b * 32 + 32] for a in range(n_a)], axis=1
             )
         )
     return jnp.concatenate(rows, axis=0)
@@ -102,8 +102,12 @@
     rows_c = jnp.concatenate([a2[pl.ds(c, 16, stride=16), :] for c in range(16)], axis=0)
     r, l = iota((128, 128), 0), iota((128, 128), 1)
     q = jnp.where((r // 64 == l // 64) & ((r % 64) // 16 == l % 4) & (r % 16 == (l % 64) // 4), 1.0, 0.0).astype(bf16)
-    spreadq = dot_nt(q, rows_c.astype(bf16))
-    tok[me_t] = swap_blocks(spreadq, 8).astype(bf16)
+    r64, l64 = iota((64, 128), 0), iota((64, 128), 1)
+    q_pair = (r64 // 32 == l64 // 64) & ((r64 % 32) // 16 == (l64 % 4) // 2) & (r64 % 16 == (l64 % 64) // 4)
+    spreadq = dot_nt(jnp.where(q_pair, 1.0, 0.0).astype(bf16), rows_c.astype(bf16))
+    tok[me_t] = jnp.concatenate(
+        [swap_blocks(spreadq, 4, 8), jnp.broadcast_to(par_row, (16, 128))], axis=0
+    ).astype(bf16)
 
     pl.semaphore_wait(barrier, n_tm - 1 + n_s - 1)
     own = pltpu.make_async_remote_copy(
@@ -127,10 +131,12 @@
 
     f, j = iota((256, 256), 0), iota((256, 256), 1)
     d = f // 32
-    source = (f % 16) * 16 + ((f // 16) % 2) * 8 + (d // 4) * 4 + d % 4
-    perm = jnp.where(j == source, 1.0, 0.0).astype(bf16)
+    column = (f % 16) * 16 + ((f // 16) % 2) * 8
+    perm = jnp.where(j == column + d, 1.0, 0.0).astype(bf16)
+    source = column + ((d // 2) % 2) * 4 + (d % 2) * 2 + d // 4
+    perm_in = jnp.where(j == source, 1.0, 0.0).astype(bf16)
     loads[2].wait()
-    wep[...] = dot(perm, we[...]).astype(bf16)
+    wep[...] = dot(perm_in, we[...]).astype(bf16)
     loads[3].wait()
     whp[:, :256] = dot_nt(wh[:, :256], perm).astype(bf16)
     whp[:, 256:] = dot_nt(wh[:, 256:], perm).astype(bf16)
@@ -149,6 +155,18 @@
     loads[7].wait()
     loads[8].wait()
 
+    lane_t = iota((TOK, 128), 1)
+    lane_bit = ((lane_t % 16) // 4 + lane_t % 4 + lane_t // 64) % 2
+    lane_sign = jnp.where(lane_bit == 0, 1.0, -1.0)
+    eye = iota((TOK, 128), 0) == lane_t
+
+    def unpack(block):
+        values = block[:TOK]
+        bits = jnp.sum(jnp.where(eye, block[TOK : TOK + 1].astype(f32), 0.0), axis=1, keepdims=True)
+        even = (1.0 - 2.0 * bits) * lane_sign > 0.0
+        wide = values.astype(f32)
+        return jnp.concatenate([jnp.where(even, wide, 0.0), jnp.where(even, 0.0, wide)], axis=1).astype(bf16)
+
     for k in range(n_c):
         here = lax.rem(chip - k + n_c, n_c)
         if k == 0:
@@ -161,7 +179,8 @@
                 sends[k].wait_recv()
                 forwards[k].start()
             forwards[k - 1].wait_recv()
-        pair = tok[pl.ds(here * 2, 2)].reshape(2 * TOK, PATCH)
+        both = [unpack(tok[here * 2]), unpack(tok[here * 2 + 1])]
+        pair = jnp.concatenate(both, axis=0)
         embedded = dot(pair, wep[...]) + b_embed
         normed = layer_norm(embedded, gain_in).astype(bf16)
         if k == 0:
@@ -207,7 +226,7 @@
     shift_tok = raw[:, 256:] + b_perm[1:2]
 
     def to_lattice(values, ref):
-        flipped = jnp.transpose(swap_blocks(values, 8))
+        flipped = jnp.transpose(swap_blocks(values, 8, 8))
         hi = flipped.astype(bf16)
         lo = (flipped - hi.astype(f32)).astype(bf16)
         ref[...] = dot(hi, q) + dot(lo, q)
@@ -261,7 +280,11 @@
     squared = field * field
     density = -2.0 * hopping * field * neighbours + squared + quartic * (squared - 1.0) * (squared - 1.0)
 
-    red_s[me_s] = jnp.concatenate([log_part, fold8(density)], axis=0)
+    logs = jnp.sum(log_part, axis=0, keepdims=True)
+    acts = jnp.sum(fold8(density), axis=0, keepdims=True)
+    red_s[me_s] = jnp.where(
+        iota((1, 128), 1) < 64, logs + pltpu.roll(logs, 64, 1), acts + pltpu.roll(acts, 64, 1)
+    )
     s_sends = [
         pltpu.make_async_remote_copy(
             src_ref=red_s.at[me_s], dst_ref=red_s.at[me_s], send_sem=rs_send.at[o - 1], recv_sem=rs_recv.at[o - 1],
@@ -297,9 +320,10 @@
     for s in t_sends:
         s.wait_recv()
     whole = jnp.sum(red_t[...], axis=0)
+    first = iota((1, 128), 1) < 64
     sites = n_s * n_tm * 256 * 128
-    tot_ref[0] = jnp.sum(whole[0:8]) / sites - 0.5 * log_two_pi
-    tot_ref[1] = jnp.sum(whole[8:16]) / sites
+    tot_ref[0] = jnp.sum(jnp.where(first, whole, 0.0)) / sites - 0.5 * log_two_pi
+    tot_ref[1] = jnp.sum(jnp.where(first, 0.0, whole)) / sites
     for s in t_sends:
         s.wait_send()
     for s in stores:
@@ -346,7 +370,7 @@
             pltpu.VMEM((256, 128), f32),
             pltpu.VMEM((256, 128), f32),
             pltpu.VMEM((256, 128), f32),
-            pltpu.VMEM((n_tm, TOK, PATCH), bf16),
+            pltpu.VMEM((n_tm, TOK + 16, 128), bf16),
             pltpu.VMEM((2 * TOK, D), f32),
             pltpu.VMEM((2 * TOK, D), bf16),
             pltpu.VMEM((TOK, D), bf16),
@@ -356,8 +380,8 @@
             pltpu.VMEM((64, 128), bf16),
             pltpu.VMEM((64, 128), bf16),
             pltpu.VMEM((64, 128), bf16),
-            pltpu.VMEM((n_s, 16, 128), f32),
-            pltpu.VMEM((n_tm, 16, 128), f32),
+            pltpu.VMEM((n_s, 1, 128), f32),
+            pltpu.VMEM((n_tm, 1, 128), f32),
             dma((9,)),
             dma((4,)),
             dma((n_c - 1,)),

time: 34.2 us -> 30.5 us (0.89)
  Pallas kernels: 33.4 us -> 29.7 us
    pallas_call x1, Pallas kernels: 31.5 us -> 27.8 us  [shards(): results = call(*extra, lattice_field, parity, *weights)]
where the time goes in v3:
time: 30.5 us; the launch traced here: 30.3 us
  Pallas kernels  29.7 us (97%)
  between operations  0.64 us (2%)
    pallas_call x1, Pallas kernels, shards(): results = call(*extra, lattice_field, parity, *weights)  27.8 us
    pallas_call x1, Pallas kernels, shards(): pl.pallas_call(write_out, out_shape=[jax.ShapeDtypeStruct(r.shape, r.dtyp...  1.93 us

profile of v3, /device:TPU:0, one launch (start us, length us, event | category | flops | bytes accessed | tf_op | source)
XLA Modules:
  0.0 30.3 jit_solution(12037560576906872686)
XLA Ops:
  0.6 27.8 %shard_map.128 = (f32[4,4,2048]{2,1,0:T(4,128)}, f32[4,4,2048]{2,1,0:T(4,128)}, f32[4,4,2048]{2,1,0:T(4,128)}, f32[4,4,2048]{2,1,0:T(4,128)}, f32[2]{0:T(128)}) custom-call(f32[4,4,2048]{2,1,0:T(4,128)} %refs_0_.1, s32[1,1,128]{2,1,0:T(1,128)} %refs_1_.1, bf16[256,768]{1,0:T(8,128)(2,1)} %refs_2_.1, f32[768]{0:T(1024)} %refs_3_.1, f32[768]{0:T(1024)} %refs_4_.1, ...), custom_call_target="tpu_custom_call" | custom-call | flops 5000000000 | bytes 6000000 | tf_op jit(solution)/shard_map/pallas_call | solution.py:404
  28.4 1.9 %shard_map.129 = (f32[4,4,2048]{2,1,0:T(4,128)}, f32[4,4,2048]{2,1,0:T(4,128)}, f32[4,4,2048]{2,1,0:T(4,128)}, f32[4,4,2048]{2,1,0:T(4,128)}, f32[2]{0:T(128)}) custom-call(f32[4,4,2048]{2,1,0:T(4,128)} %get-tuple-element.10.refs_0_, f32[4,4,2048]{2,1,0:T(4,128)} %get-tuple-element.11.refs_1_, f32[4,4,2048]{2,1,0:T(4,128)} %get-tuple-element.12.refs_2_, ...), custom_call_target="tpu_custom_call" | custom-call | bytes 1048576 | tf_op jit(solution)/shard_map/pallas_call | solution.py:405
